TPU v7x, 128 devices: a whole 4x4x4 slice. The times are simulated.
128 devices in a mesh: batch: 8 (over y, core), blk: 16 (over x, z).
Axes of the slice: x: 4, y: 4, z: 4, core: 2. Of those that a mesh axis runs over, the one named last changes fastest.
Arguments:
- inputs: bfloat16 [8, 2048, 768], P('batch', 'blk'), may hold values from -6 to 6
- queries: bfloat16 [8, 2048, 768], P('batch', 'blk'), may hold values from -6 to 6
- lengths: int32 [8], P('batch'), may hold values from 1921 to 2048, as said below
- latent_array: bfloat16 [256, 1280], P('blk'), may hold values from -6 to 6
- latent_mats: bfloat16 [10, 1280, 1280], P(None, 'blk'), may hold values from -0.15625 to 0.15625
- out_mats: bfloat16 [2, 1280, 1280], P(None, 'blk'), may hold values from -0.75 to 0.75
- byte_mats: bfloat16 [3, 768, 1280], P(None, 'blk'), may hold values from -0.21875 to 0.21875
- dec_out: bfloat16 [1280, 768], P('blk'), may hold values from -0.75 to 0.75
- latent_gains: float32 [5, 1280], replicated, may hold values from 0.5 to 1.5
- byte_gains: float32 [2, 768], replicated, may hold values from 0.5 to 1.5
- cotangent: bfloat16 [8, 2048, 768], P('batch', 'blk'), may hold values from -6 to 6
Outputs:
- result: bfloat16 [8, 2048, 768], P('batch', 'blk')
- grad_inputs: float32 [8, 2048, 768], P('batch', 'blk')
- grad_queries: float32 [8, 2048, 768], P('batch', 'blk')
- grad_latent_array: float32 [256, 1280], P('batch', 'blk')
- grad_latent_mats: float32 [10, 1280, 1280], P(None, 'batch', 'blk')
- grad_out_mats: float32 [2, 1280, 1280], P(None, 'batch', 'blk')
- grad_byte_mats: float32 [3, 768, 1280], P(None, 'batch', 'blk')
- grad_dec_out: float32 [1280, 768], P('batch', 'blk')
- grad_latent_gains: float32 [5, 1280], replicated
- grad_byte_gains: float32 [2, 768], replicated
Inputs may be any that keep to these rules, and one draw needn't show every extreme that they name: `lengths`: byte positions at or past a sequence's length are padding whose keys are masked; every draw has a sequence of length 2048.
All inputs are finite; a program needn't handle non-finite values.
Results may differ from a plain program's by a relative error of at most 0.025.
Values may be sent and summed in bfloat16 or wider, within the bound.
No kernel may reach another device: no remote copies, remote signals or barrier semaphores. Data moves between devices by JAX's collectives and lax.ppermute only.
A program may use at most 256 MiB of HBM per device.

v0:
```python
import jax
import jax.numpy as jnp
from jax import lax
from jax.sharding import PartitionSpec as P

HEADS = 8


EPSILON = 1e-05


def matmul(left_op, right_op):
    return jnp.dot(left_op, right_op, preferred_element_type=jnp.float32)


def matmul_tn(left_op, right_op):
    return jnp.dot(left_op.T, right_op, preferred_element_type=jnp.float32)


def matmul_nt(left_op, right_op):
    return jnp.dot(left_op, right_op.T, preferred_element_type=jnp.float32)


def to_half(values):
    return values.astype(jnp.bfloat16)


def norm_forward(values, gain_vec):
    center = values - jnp.mean(values, axis=-1, keepdims=True)
    spread = jnp.mean(center * center, axis=-1, keepdims=True)
    inverse = lax.rsqrt(spread + EPSILON)
    normed = center * inverse
    return (normed * gain_vec, (normed, inverse))


def norm_backward(grad_in, gain_vec, saved):
    normed, inverse = saved
    gain_grad = jnp.sum(grad_in * normed, axis=0)
    inner = grad_in * gain_vec
    first_mean = jnp.mean(inner, axis=-1, keepdims=True)
    second_mean = jnp.mean(inner * normed, axis=-1, keepdims=True)
    return (inverse * (inner - first_mean - normed * second_mean), gain_grad)


def gelu_backward(pre_act, grad_act):
    unused, pull_back = jax.vjp(jax.nn.gelu, pre_act)
    return pull_back(grad_act)[0]


def split_heads(values):
    return values.reshape(values.shape[0], HEADS, -1)


def scale_of(values):
    return (values.shape[1] // HEADS) ** (-0.5)


def score_block(query_b, key_b, valid_keys):
    scores = jnp.einsum(
        "mhe,nhe->hmn", split_heads(query_b), split_heads(key_b), preferred_element_type=jnp.float32
    ) * scale_of(query_b)
    return jnp.where(valid_keys[None, None, :], scores, -1e30)


def softmax_stats(scores):
    row_peak = jnp.max(scores, axis=-1, keepdims=True)
    row_total = jnp.sum(jnp.exp(scores - row_peak), axis=-1, keepdims=True)
    return (row_peak, row_total)


def probabilities(scores, row_peak, row_total):
    return jnp.exp(scores - row_peak) / row_total


def mix_values(probability, value_b):
    mixture = jnp.einsum(
        "hmn,nhe->mhe",
        to_half(probability),
        split_heads(value_b),
        preferred_element_type=jnp.float32,
    )
    return mixture.reshape(mixture.shape[0], -1)


def value_prob_grad(grad_mix_b, value_b):
    return jnp.einsum(
        "mhe,nhe->hmn",
        split_heads(grad_mix_b),
        split_heads(value_b),
        preferred_element_type=jnp.float32,
    )


def query_grad(score_b, key_b):
    grads = jnp.einsum(
        "hmn,nhe->mhe", score_b, split_heads(key_b), preferred_element_type=jnp.float32
    ) * scale_of(key_b)
    return grads.reshape(grads.shape[0], -1)


def key_grad(score_b, query_b):
    grads = jnp.einsum(
        "hmn,mhe->nhe", score_b, split_heads(query_b), preferred_element_type=jnp.float32
    ) * scale_of(query_b)
    return grads.reshape(grads.shape[0], -1)


def value_grad(probability, grad_mix_b):
    grads = jnp.einsum(
        "hmn,mhe->nhe",
        to_half(probability),
        split_heads(grad_mix_b),
        preferred_element_type=jnp.float32,
    )
    return grads.reshape(grads.shape[0], -1)


def attention_backward(query_b, key_b, value_b, probability, grad_mix_b):
    dprob = value_prob_grad(grad_mix_b, value_b)
    row_dot = jnp.sum(probability * dprob, axis=-1, keepdims=True)
    score_b = to_half(probability * (dprob - row_dot))
    return (
        query_grad(score_b, key_b),
        key_grad(score_b, query_b),
        value_grad(probability, grad_mix_b),
    )


def shards(
    inputs,
    queries,
    lengths,
    latent_array,
    latent_mats,
    out_mats,
    byte_mats,
    dec_out,
    latent_gains,
    byte_gains,
    cotangent,
):
    lat_full, mats_full, outs_full, bytes_full, dec_full = (
        lax.all_gather(latent_array, "blk", axis=0, tiled=True),
        lax.all_gather(latent_mats, "blk", axis=1, tiled=True),
        lax.all_gather(out_mats, "blk", axis=1, tiled=True),
        lax.all_gather(byte_mats, "blk", axis=1, tiled=True),
        lax.all_gather(dec_out, "blk", axis=0, tiled=True),
    )
    block_index = lax.axis_index("blk")
    block_count = lax.axis_size("blk")
    own_rows = inputs.shape[1]
    own_start = block_index * own_rows
    seq_length = lengths[0]
    latent_valid = jnp.ones((lat_full.shape[0],), bool)
    col_width = mats_full.shape[2] // block_count
    col_start = block_index * col_width

    def own_cols(values):
        return lax.dynamic_slice_in_dim(values, col_start, col_width, 1)

    byte_in = inputs[0].astype(jnp.float32)
    normed_in, saved_in = norm_forward(byte_in, byte_gains[0])
    normed_in_b = to_half(normed_in)
    key_b = to_half(matmul(normed_in_b, bytes_full[0]))
    value_b = to_half(matmul(normed_in_b, bytes_full[1]))
    latent_zero = lat_full.astype(jnp.float32)
    normed_q, saved_q = norm_forward(latent_zero, latent_gains[0])
    normed_q_b = to_half(normed_q)
    query_e = to_half(matmul(normed_q_b, mats_full[0]))
    all_keys, all_values = (
        lax.all_gather(key_b, "blk", axis=0, tiled=True),
        lax.all_gather(value_b, "blk", axis=0, tiled=True),
    )
    every_valid = jnp.arange(all_keys.shape[0], dtype=jnp.int32) < seq_length
    enc_scores = score_block(query_e, all_keys, every_valid)
    enc_peak, enc_total = softmax_stats(enc_scores)
    enc_mix = mix_values(probabilities(enc_scores, enc_peak, enc_total), all_values)
    mix_e_b = to_half(enc_mix)
    latent_one = latent_zero + matmul(mix_e_b, outs_full[0])
    normed_f1, saved_f1 = norm_forward(latent_one, latent_gains[1])
    normed_f1_b = to_half(normed_f1)
    hidden_one = matmul(normed_f1_b, mats_full[1])
    active_one_b = to_half(jax.nn.gelu(hidden_one))
    latent_two = latent_one + matmul(active_one_b, mats_full[2])
    normed_s, saved_s = norm_forward(latent_two, latent_gains[2])
    normed_s_b = to_half(normed_s)
    query_s = to_half(matmul(normed_s_b, mats_full[3]))
    key_s = to_half(matmul(normed_s_b, mats_full[4]))
    value_s = to_half(matmul(normed_s_b, mats_full[5]))
    scores_s = score_block(query_s, key_s, latent_valid)
    peak_s, total_s = softmax_stats(scores_s)
    prob_s = probabilities(scores_s, peak_s, total_s)
    mix_s_b = to_half(mix_values(prob_s, value_s))
    latent_three = latent_two + matmul(mix_s_b, outs_full[1])
    normed_f2, saved_f2 = norm_forward(latent_three, latent_gains[3])
    normed_f2_b = to_half(normed_f2)
    hidden_two = matmul(normed_f2_b, mats_full[6])
    active_two_b = to_half(jax.nn.gelu(hidden_two))
    latent_four = latent_three + matmul(active_two_b, mats_full[7])
    normed_c, saved_c = norm_forward(latent_four, latent_gains[4])
    normed_c_b = to_half(normed_c)
    key_d = to_half(matmul(normed_c_b, mats_full[8]))
    value_d = to_half(matmul(normed_c_b, mats_full[9]))
    byte_query = queries[0].astype(jnp.float32)
    normed_d, saved_d = norm_forward(byte_query, byte_gains[1])
    normed_d_b = to_half(normed_d)
    query_d = to_half(matmul(normed_d_b, bytes_full[2]))
    scores_d = score_block(query_d, key_d, latent_valid)
    peak_d, total_d = softmax_stats(scores_d)
    prob_d = probabilities(scores_d, peak_d, total_d)
    mix_d_b = to_half(mix_values(prob_d, value_d))
    output_rows = byte_query + matmul(mix_d_b, dec_full)
    grad_out = cotangent[0].astype(jnp.float32)
    grad_out_b = to_half(grad_out)
    grad_dec = matmul_tn(mix_d_b, grad_out_b)
    grad_mix_d = to_half(matmul_nt(grad_out_b, dec_full))
    grad_query_d, grad_key_d, grad_value_d = attention_backward(
        query_d, key_d, value_d, prob_d, grad_mix_d
    )
    grad_query_d_b = to_half(grad_query_d)
    grad_in_d, gain_grad_d = norm_backward(
        matmul_nt(grad_query_d_b, bytes_full[2]), byte_gains[1], saved_d
    )
    grad_queries = grad_out + grad_in_d
    sum_key_d, sum_value_d = (
        lax.psum(grad_key_d.astype(jnp.bfloat16), "blk").astype(jnp.float32),
        lax.psum(grad_value_d.astype(jnp.bfloat16), "blk").astype(jnp.float32),
    )
    sum_key_b = to_half(sum_key_d)
    sum_value_b = to_half(sum_value_d)
    grad_mat_kd = matmul_tn(normed_c_b, own_cols(sum_key_b))
    grad_mat_vd = matmul_tn(normed_c_b, own_cols(sum_value_b))
    grad_normed_c = matmul_nt(sum_key_b, mats_full[8]) + matmul_nt(sum_value_b, mats_full[9])
    grad_four, gain_grad_c = norm_backward(grad_normed_c, latent_gains[4], saved_c)
    grad_four_b = to_half(grad_four)
    grad_mat_f2out = matmul_tn(active_two_b, own_cols(grad_four_b))
    grad_hidden_two = to_half(gelu_backward(hidden_two, matmul_nt(grad_four_b, mats_full[7])))
    grad_mat_f2in = matmul_tn(normed_f2_b, own_cols(grad_hidden_two))
    grad_norm_f2, gain_grad_f2 = norm_backward(
        matmul_nt(grad_hidden_two, mats_full[6]), latent_gains[3], saved_f2
    )
    grad_three = grad_four + grad_norm_f2
    grad_three_b = to_half(grad_three)
    grad_out_s = matmul_tn(mix_s_b, own_cols(grad_three_b))
    grad_mix_s = to_half(matmul_nt(grad_three_b, outs_full[1]))
    grad_query_s, grad_key_s, grad_value_s = attention_backward(
        query_s, key_s, value_s, prob_s, grad_mix_s
    )
    grad_query_s_b = to_half(grad_query_s)
    grad_key_s_b = to_half(grad_key_s)
    grad_value_s_b = to_half(grad_value_s)
    grad_mat_qs = matmul_tn(normed_s_b, own_cols(grad_query_s_b))
    grad_mat_ks = matmul_tn(normed_s_b, own_cols(grad_key_s_b))
    grad_mat_vs = matmul_tn(normed_s_b, own_cols(grad_value_s_b))
    grad_normed_s = (
        matmul_nt(grad_query_s_b, mats_full[3])
        + matmul_nt(grad_key_s_b, mats_full[4])
        + matmul_nt(grad_value_s_b, mats_full[5])
    )
    grad_norm_s, gain_grad_s = norm_backward(grad_normed_s, latent_gains[2], saved_s)
    grad_two = grad_three + grad_norm_s
    grad_two_b = to_half(grad_two)
    grad_mat_f1out = matmul_tn(active_one_b, own_cols(grad_two_b))
    grad_hidden_one = to_half(gelu_backward(hidden_one, matmul_nt(grad_two_b, mats_full[2])))
    grad_mat_f1in = matmul_tn(normed_f1_b, own_cols(grad_hidden_one))
    grad_norm_f1, gain_grad_f1 = norm_backward(
        matmul_nt(grad_hidden_one, mats_full[1]), latent_gains[1], saved_f1
    )
    grad_one = grad_two + grad_norm_f1
    grad_one_b = to_half(grad_one)
    grad_out_e = matmul_tn(mix_e_b, own_cols(grad_one_b))
    grad_mix_e = to_half(matmul_nt(grad_one_b, outs_full[0]))
    enc_prob = probabilities(score_block(query_e, all_keys, every_valid), enc_peak, enc_total)
    dprob_e = value_prob_grad(grad_mix_e, all_values)
    row_dot = jnp.sum(enc_prob * dprob_e, axis=-1, keepdims=True)
    score_all_b = to_half(enc_prob * (dprob_e - row_dot))
    grad_query_e = query_grad(score_all_b, all_keys)
    own_scores = lax.dynamic_slice_in_dim(score_all_b, own_start, own_rows, 2)
    own_prob = lax.dynamic_slice_in_dim(enc_prob, own_start, own_rows, 2)
    grad_query_e_b = to_half(grad_query_e)
    grad_mat_qe = matmul_tn(normed_q_b, own_cols(grad_query_e_b))
    grad_norm_q, gain_grad_q = norm_backward(
        matmul_nt(grad_query_e_b, mats_full[0]), latent_gains[0], saved_q
    )
    grad_latent = grad_one + grad_norm_q
    grad_key_b = to_half(key_grad(own_scores, query_e))
    grad_value_b = to_half(value_grad(own_prob, grad_mix_e))
    grad_normed_in = matmul_nt(grad_key_b, bytes_full[0]) + matmul_nt(grad_value_b, bytes_full[1])
    grad_inputs, gain_grad_in = norm_backward(grad_normed_in, byte_gains[0], saved_in)
    lat_grads = jnp.stack(
        [
            grad_mat_qe,
            grad_mat_f1in,
            grad_mat_f1out,
            grad_mat_qs,
            grad_mat_ks,
            grad_mat_vs,
            grad_mat_f2in,
            grad_mat_f2out,
            grad_mat_kd,
            grad_mat_vd,
        ]
    )
    outs_grads = jnp.stack([grad_out_e, grad_out_s])
    array_piece = own_cols(grad_latent)[None]
    sum_array, sum_mats, sum_outs = (
        lax.psum_scatter(
            array_piece.astype(jnp.bfloat16), "batch", scatter_dimension=1, tiled=True
        ).astype(jnp.float32),
        lax.psum_scatter(
            lat_grads.astype(jnp.bfloat16), "batch", scatter_dimension=1, tiled=True
        ).astype(jnp.float32),
        lax.psum_scatter(
            outs_grads.astype(jnp.bfloat16), "batch", scatter_dimension=1, tiled=True
        ).astype(jnp.float32),
    )
    bytes_grads = jnp.stack(
        [
            matmul_tn(normed_in_b, grad_key_b),
            matmul_tn(normed_in_b, grad_value_b),
            matmul_tn(normed_d_b, grad_query_d_b),
        ]
    )
    bytes_cols, dec_cols = (
        lax.psum_scatter(
            bytes_grads.astype(jnp.bfloat16), "blk", scatter_dimension=2, tiled=True
        ).astype(jnp.float32),
        lax.psum_scatter(
            grad_dec[None].astype(jnp.bfloat16), "blk", scatter_dimension=2, tiled=True
        ).astype(jnp.float32),
    )
    bytes_rows, dec_rows = (
        lax.psum_scatter(
            bytes_cols.astype(jnp.bfloat16), "batch", scatter_dimension=1, tiled=True
        ).astype(jnp.float32),
        lax.psum_scatter(
            dec_cols.astype(jnp.bfloat16), "batch", scatter_dimension=1, tiled=True
        ).astype(jnp.float32),
    )
    lat_gain_terms = jnp.where(
        block_index == 0,
        jnp.stack([gain_grad_q, gain_grad_f1, gain_grad_s, gain_grad_f2, gain_grad_c]),
        0.0,
    )
    byte_gain_terms = jnp.stack([gain_grad_in, gain_grad_d])
    gain_lat, gain_byte = lax.psum((lat_gain_terms, byte_gain_terms), ("batch", "blk"))
    return (
        to_half(output_rows)[None],
        grad_inputs[None],
        grad_queries[None],
        sum_array[0],
        sum_mats,
        sum_outs,
        bytes_rows,
        dec_rows[0],
        gain_lat,
        gain_byte,
    )


def solution(mesh):
    return jax.shard_map(
        shards,
        mesh=mesh,
        in_specs=(
            P("batch", "blk", None),
            P("batch", "blk", None),
            P("batch"),
            P("blk", None),
            P(None, "blk", None),
            P(None, "blk", None),
            P(None, "blk", None),
            P("blk", None),
            P(),
            P(),
            P("batch", "blk", None),
        ),
        out_specs=(
            P("batch", "blk", None),
            P("batch", "blk", None),
            P("batch", "blk", None),
            P("batch", "blk"),
            P(None, "batch", "blk"),
            P(None, "batch", "blk"),
            P(None, "batch", "blk"),
            P("batch", "blk"),
            P(),
            P(),
        ),
        check_vma=False,
    )
```

profile of v0, /device:TPU:1, one launch (start us, length us, event | category | flops | bytes accessed | tf_op | source)
XLA Modules:
  0.0 1099.7 jit_solution(2075396443979131011)
XLA Ops:
  11.7 61.3 %all-gather.7.cloned.1.call-done = bf16[3,768,1280]{2,1,0:T(8,128)(2,1)} async-done(((bf16[3,48,1280]{2,1,0:T(8,128)(2,1)}), bf16[3,768,1280]{2,1,0:T(8,128)(2,1)}) %all-gather.7.cloned.1.call-update) | async-done | bytes 5898256 | tf_op jit(solution)/shard_map/all_gather | solution.py:146
  81.2 19.9 %all_gather.21 = bf16[256,1280]{1,0:T(8,128)(2,1)S(1)} all-gather(bf16[16,1280]{1,0:T(8,128)(2,1)S(1)} %copy-done.49), channel_id=1, replica_groups=mesh['batch'=8,'blk'=16] {'blk'}, dimensions={0}, use_global_device_ids=true | all-gather | bytes 696320 | tf_op jit(solution)/shard_map/all_gather | solution.py:143
  101.7 17.4 %all-gather.17.cloned.1.call-done = bf16[1280,768]{1,0:T(8,128)(2,1)} async-done(((bf16[80,768]{1,0:T(8,128)(2,1)}), bf16[1280,768]{1,0:T(8,128)(2,1)}) %all-gather.17.cloned.1.call-update) | async-done | bytes 1966096 | tf_op jit(solution)/shard_map/all_gather | solution.py:147
  125.2 53.2 %all-gather.13.cloned.1.call-done = bf16[2048,1280]{1,0:T(8,128)(2,1)} async-done(((bf16[128,1280]{1,0:T(8,128)(2,1)}), bf16[2048,1280]{1,0:T(8,128)(2,1)}) %all-gather.13.cloned.1.call-update) | async-done | bytes 5242896 | tf_op jit(solution)/shard_map/all_gather | solution.py:171
  186.3 50.7 %all-gather.9.cloned.1.call-done = bf16[2048,1280]{1,0:T(8,128)(2,1)} async-done(((bf16[128,1280]{1,0:T(8,128)(2,1)}), bf16[2048,1280]{1,0:T(8,128)(2,1)}) %all-gather.9.cloned.1.call-update) | async-done | bytes 5242896 | tf_op jit(solution)/shard_map/all_gather | solution.py:172
  245.0 186.9 %all-gather.11.cloned.1.call-done = bf16[10,1280,1280]{2,1,0:T(8,128)(2,1)} async-done(((bf16[10,80,1280]{2,1,0:T(8,128)(2,1)}), bf16[10,1280,1280]{2,1,0:T(8,128)(2,1)}) %all-gather.11.cloned.1.call-update) | async-done | bytes 32768016 | tf_op jit(solution)/shard_map/all_gather | solution.py:144
  435.1 10.8 fusion.202
  446.0 12.1 %broadcast_divide_fusion = f32[8,256,2048]{2,1,0:T(8,128)} fusion(f32[8,256,2048]{2,1,0:T(8,128)} %get-tuple-element.95, f32[8,256]{1,0:T(8,128)S(1)} %get-tuple-element.94), kind=kLoop, calls=%fused_computation.11 | loop fusion | flops 4194304 | bytes 33562624 | tf_op jit(solution)/shard_map/div | solution.py:72
  458.0 10.3 fusion.86
  468.3 27.7 %all-gather.15.cloned.1.call-done = bf16[2,1280,1280]{2,1,0:T(8,128)(2,1)} async-done(((bf16[2,80,1280]{2,1,0:T(8,128)(2,1)}), bf16[2,1280,1280]{2,1,0:T(8,128)(2,1)}) %all-gather.15.cloned.1.call-update) | async-done | bytes 6553616 | tf_op jit(solution)/shard_map/all_gather | solution.py:145
  568.0 9.3 copy.111
  581.8 66.5 %all-reduce.10.cloned.1.call-done = (bf16[256,1280]{0,1:T(8,128)(2,1)}, bf16[256,1280]{0,1:T(8,128)(2,1)}) async-done(((bf16[256,1280]{0,1:T(8,128)(2,1)}, bf16[256,1280]{0,1:T(8,128)(2,1)}), (bf16[256,1280]{0,1:T(8,128)(2,1)}, bf16[256,1280]{0,1:T(8,128)(2,1)})) %all-reduce.10.cloned.1.call-update) | async-done | bytes 1310736 | tf_op jit(solution)/shard_map/psum | solution.py:227
  702.3 15.9 %multiply_reduce_fusion = (f32[8,256]{1,0:T(8,128)S(1)}, f32[8,256,2048]{2,1,0:T(8,128)}) fusion(f32[8,256,2048]{2,1,0:T(8,128)} %broadcast_divide_fusion, bf16[256,8,160]{0,2,1:T(8,128)(2,1)} %bitcast.402, bf16[2048,8,160]{0,2,1:T(8,128)(2,1)} %bitcast.395), kind=kOutput, calls=%fused_computation.4 | convolution fusion | flops 1350563840 | bytes 39460864 | tf_op jit(solution)/shard_map/mhe,nhe->hmn/dot_general | solution.py:86
  719.7 11.6 %multiply_convert_fusion = bf16[8,256,2048]{2,1,0:T(8,128)(2,1)S(1)} fusion(f32[8,256,2048]{2,1,0:T(8,128)} %get-tuple-element.117, f32[8,256]{1,0:T(8,128)S(1)} %get-tuple-element.116, f32[8,256,2048]{2,1,0:T(8,128)} %get-tuple-element.95, f32[8,256]{1,0:T(8,128)S(1)} %get-tuple-element.94), kind=kLoop, calls=%fused_computation.3 | loop fusion | flops 16777216 | bytes 41959424 | tf_op jit(solution)/shard_map/convert_element_type | solution.py:25
  740.6 12.7 %copy.110 = bf16[3,768,1280]{1,0,2:T(4,128)(2,1)} copy(bf16[3,768,1280]{2,1,0:T(8,128)(2,1)} %pad_maximum_fusion) | data formatting | bytes 11796480 | tf_op jit(solution)/shard_map/stack | solution.py:317
  758.0 8.4 fusion.83
  800.6 8.0 reshape.401
  820.3 105.4 %all-reduce.8.cloned.1.call-done = (bf16[3,768,1280]{1,0,2:T(4,128)(2,1)}, bf16[1,1280,768]{1,0,2:T(2,128)(2,1)}) async-done(((bf16[3,768,1280]{1,0,2:T(4,128)(2,1)}, bf16[1,1280,768]{1,0,2:T(2,128)(2,1)}), (bf16[3,768,1280]{1,0,2:T(4,128)(2,1)}, bf16[1,1280,768]{1,0,2:T(2,128)(2,1)})) %all-reduce.8.cloned.1.call-update) | async-done | bytes 7864336
  926.9 12.7 %copy.125 = bf16[1,1280,48]{0,2,1:T(8,128)(2,1)} copy(bf16[1,1280,48]{1,0,2:T(2,128)(2,1)S(1)} %constant_dynamic-slice_fusion) | data formatting | bytes 245760
  939.6 12.7 %bitcast_reduce_fusion = bf16[1280,48]{1,0:T(8,128)(2,1)} fusion(bf16[1,1280,48]{0,2,1:T(8,128)(2,1)} %copy.125), kind=kLoop, calls=%fused_computation.7 | loop fusion | bytes 245760
  953.7 11.2 %copy.123 = bf16[3,768,80]{0,2,1:T(8,128)(2,1)} copy(bf16[3,768,80]{1,0,2:T(4,128)(2,1)S(1)} %constant_dynamic-slice_fusion.1) | data formatting | bytes 737280
  964.9 16.9 %reshape.405 = bf16[768,240]{1,0:T(8,128)(2,1)} reshape(bf16[768,80,3]{2,1,0:T(8,128)(2,1)} %bitcast.393) | data formatting | bytes 737280
  981.9 66.0 %all-reduce.2 = (f32[5,1280]{1,0:T(8,128)}, f32[2,768]{1,0:T(2,128)}) all-reduce(f32[5,1280]{1,0:T(8,128)S(1)} %broadcast_select_fusion, f32[2,768]{1,0:T(2,128)S(1)} %pad_maximum_fusion.2), channel_id=1, replica_groups=mesh['batch'=8,'blk'=16] {'batch','blk'}, use_global_device_ids=true, to_apply=%region_51.52 | all-reduce | flops 7936 | bytes 63488 | tf_op jit(solution)/shard_map/psum | solution.py:346
  1063.0 24.8 %reduce-scatter.20.cloned.1.call-done = bf16[96,240]{1,0:T(8,128)(2,1)} async-done(((bf16[768,240]{1,0:T(8,128)(2,1)}), bf16[96,240]{1,0:T(8,128)(2,1)}) %reduce-scatter.20.cloned.1.call-update) | async-done | bytes 46096
  (363 shorter events, 249.4 us)
Async XLA Ops:
  7.2 65.8 %all-gather.7.cloned.1.call-start = ((), (), s32[]{:S(2)}) async-start(), calls=%async_computation.5 | async-start | bytes 6266880 | tf_op jit(solution)/shard_map/all_gather | solution.py:146
  7.9 111.2 %all-gather.17.cloned.1.call-start = ((), (), s32[]{:S(2)}) async-start(), calls=%async_computation.10 | async-start | bytes 2088960 | tf_op jit(solution)/shard_map/all_gather | solution.py:147
  8.7 169.7 %all-gather.13.cloned.1.call-start = ((), (), s32[]{:S(2)}) async-start(), calls=%async_computation.8 | async-start | bytes 5570560 | tf_op jit(solution)/shard_map/all_gather | solution.py:171
  10.5 65.4 %copy-start.54 = (f32[128]{0:T(128)}, f32[128]{0:T(128)S(1)}, u32[]{:S(2)}) copy-start(f32[128]{0:T(128)S(1)} %broadcast_multiply_fusion.21) | copy-start | bytes 1540
  11.7 64.3 %copy-start.62 = (f32[128]{0:T(128)}, f32[128]{0:T(128)S(1)}, u32[]{:S(2)}) copy-start(f32[128]{0:T(128)S(1)} %add_rsqrt_fusion.6) | copy-start | bytes 1540
  75.9 161.1 %all-gather.9.cloned.1.call-start = ((), (), s32[]{:S(2)}) async-start(), calls=%async_computation.6 | async-start | bytes 5570560 | tf_op jit(solution)/shard_map/all_gather | solution.py:172
  78.8 353.0 %all-gather.11.cloned.1.call-start = ((), (), s32[]{:S(2)}) async-start(), calls=%async_computation.7 | async-start | bytes 34816000 | tf_op jit(solution)/shard_map/all_gather | solution.py:144
  79.4 416.6 %all-gather.15.cloned.1.call-start = ((), (), s32[]{:S(2)}) async-start(), calls=%async_computation.9 | async-start | bytes 6963200 | tf_op jit(solution)/shard_map/all_gather | solution.py:145
  80.0 39.1 %copy-start.29 = (bf16[1,128,768]{2,1,0:T(8,128)(2,1)S(1)}, bf16[1,128,768]{2,1,0:T(8,128)(2,1)}, u32[]{:S(2)}) copy-start(bf16[1,128,768]{2,1,0:T(8,128)(2,1)} %param.21) | copy-start | bytes 589828
  80.0 568.2 %all-reduce.10.cloned.1.call-start = ((), (), s32[]{:S(2)}) async-start(), calls=%async_computation.17 | async-start | bytes 2621440 | tf_op jit(solution)/shard_map/psum | solution.py:227
  80.9 351.0 %copy-start.58 = (f32[1280]{0:T(1024)}, f32[1280]{0:T(1024)S(1)}, u32[]{:S(2)}) copy-start(f32[1280]{0:T(1024)S(1)} %get-tuple-element.74) | copy-start | bytes 15364
  81.0 41.3 %copy-start.64 = (f32[128]{0:T(128)}, f32[128]{0:T(128)S(1)}, u32[]{:S(2)}) copy-start(f32[128]{0:T(128)S(1)} %broadcast_multiply_fusion.20) | copy-start | bytes 1540
  101.1 394.9 %copy-start.8 = (bf16[256,1280]{1,0:T(8,128)(2,1)}, bf16[256,1280]{1,0:T(8,128)(2,1)S(1)}, u32[]{:S(2)}) copy-start(bf16[256,1280]{1,0:T(8,128)(2,1)S(1)} %all_gather.21) | copy-start | bytes 1966084
  101.3 330.5 %copy-start.67 = (f32[256]{0:T(256)}, f32[256]{0:T(256)S(1)}, u32[]{:S(2)}) copy-start(f32[256]{0:T(256)S(1)} %broadcast_multiply_fusion.15) | copy-start | bytes 3076
  101.7 20.6 %copy-start.73 = (f32[128]{0:T(128)}, f32[128]{0:T(128)S(1)}, u32[]{:S(2)}) copy-start(f32[128]{0:T(128)S(1)} %add_rsqrt_fusion.5) | copy-start | bytes 1540
  101.7 330.2 %copy-start.69 = (f32[256]{0:T(256)}, f32[256]{0:T(256)S(1)}, u32[]{:S(2)}) copy-start(f32[256]{0:T(256)S(1)} %add_rsqrt_fusion.4) | copy-start | bytes 3076
  468.3 30.8 %copy-start.21 = (bf16[8,160,256]{2,1,0:T(8,128)(2,1)}, bf16[8,160,256]{2,1,0:T(8,128)(2,1)S(1)}, u32[]{:S(2)}) copy-start(bf16[8,160,256]{2,1,0:T(8,128)(2,1)S(1)} %fusion.86) | copy-start | bytes 1966084
  561.9 363.7 %all-reduce.8.cloned.1.call-start = ((), (), s32[]{:S(2)}) async-start(), calls=%async_computation.16 | async-start | bytes 23592960
  753.2 295.8 %reduce-scatter.14.cloned.1.call-start = ((), (), s32[]{:S(2)}) async-start(), calls=%async_computation.11 | async-start | bytes 73728 | tf_op jit(solution)/shard_map/reduce_scatter | solution.py:307
  783.7 266.6 %reduce-scatter.18.cloned.1.call-start = ((), (), s32[]{:S(2)}) async-start(), calls=%async_computation.13 | async-start | bytes 737280
  785.6 266.6 %reduce-scatter.16.cloned.1.call-start = ((), (), s32[]{:S(2)}) async-start(), calls=%async_computation.12 | async-start | bytes 2580480
  808.7 247.1 %reduce-scatter.22.cloned.1.call-start = ((), (), s32[]{:S(2)}) async-start(), calls=%async_computation.15 | async-start | bytes 368640
  952.4 135.4 %reduce-scatter.20.cloned.1.call-start = ((), (), s32[]{:S(2)}) async-start(), calls=%async_computation.14 | async-start | bytes 442368
  964.9 82.9 %copy-start.30 = (bf16[1,128,768]{2,1,0:T(8,128)(2,1)S(1)}, bf16[1,128,768]{2,1,0:T(8,128)(2,1)}, u32[]{:S(2)}) copy-start(bf16[1,128,768]{2,1,0:T(8,128)(2,1)} %param.21) | copy-start | bytes 589828
  (77 other events, 303.7 us)
Sparse Core Ops, SparseCore 0:
  10.1 62.7 all-gather.6
  75.2 43.8 all-gather.16
  121.8 56.4 all-gather.12
  181.0 56.0 all-gather.8
  239.1 192.7 all-gather.10
  433.8 62.1 all-gather.14
  562.1 86.1 all-reduce.9
  753.4 172.2 all-reduce.7
  928.7 27.3 reduce-scatter.13
  958.4 29.8 reduce-scatter.17
  990.7 32.8 reduce-scatter.15
  1025.8 29.9 reduce-scatter.21
  1058.3 29.5 reduce-scatter.19
where the time goes:
time: 1110 us; the launch traced here: 1100 us
  waiting for transfers between devices  597 us (54%)
  matrix products  201 us (18%)
  local copies, waits for them, and re-layouts  154 us (14%)
  blocking collectives  85.9 us (8%)
  other arithmetic  43.8 us (4%)
  between operations  17.8 us (2%)
    all_gather x1, waiting for transfers between devices, shards(): lax.all_gather(latent_mats, 'blk', axis=1, tiled=True)  187 us
    unnamed x18, waiting for transfers between devices  133 us
    unnamed x198, local copies, waits for them, and re-layouts  101 us
    psum x1, waiting for transfers between devices, shards(): lax.psum(grad_value_d.astype(jnp.bfloat16), 'blk').astype(jnp.float32)  66.5 us
    psum x1, blocking collectives, shards(): lax.psum((lat_gain_terms, byte_gain_terms), ('batch', 'blk'))  66 us
    all_gather x1, waiting for transfers between devices, shards(): lax.all_gather(byte_mats, 'blk', axis=1, tiled=True)  61.3 us
    all_gather x1, waiting for transfers between devices, shards(): lax.all_gather(key_b, 'blk', axis=0, tiled=True)  53.2 us
    all_gather x1, waiting for transfers between devices, shards(): lax.all_gather(value_b, 'blk', axis=0, tiled=True)  50.7 us
  transfers between devices with their start and end apart: 13, of which 10 were waited for; matrix products, arithmetic and copies ran while one was open for 20% of the time, Pallas kernels for 0%

commit v1 on v0

v1 whole, which is shorter than its diff:
```python
import jax
import jax.numpy as jnp
from jax import lax
from jax.experimental import pallas as pl
from jax.experimental.pallas import tpu as pltpu
from jax.sharding import Mesh, PartitionSpec as P

F32, BF = jnp.float32, jnp.bfloat16
D, DI, R, N, H, E = 1280, 768, 256, 128, 8, 160
NX, NZ, NJ, NI = 4, 4, 16, 8
SCALE = E**-0.5
EPS = 1e-5
MIB = 1 << 20
AXES = ("y", "core", "x", "z")
BATCH = ("y", "core")
BLK = ("x", "z")
WIN = [128 * (E * h // 128) for h in range(H)]
OFF = [E * h - WIN[h] for h in range(H)]
SQUARE = [("o", 0), ("l", 1), ("l", 2), ("l", 3), ("l", 4), ("l", 5), ("o", 1), ("l", 6), ("l", 7), ("l", 8), ("l", 9)]
ROWS_I = 128
DEC_ROW, BQ_ROW = 880, 960


def dot(a, b, ca=1, cb=0):
    return lax.dot_general(a, b, (((ca,), (cb,)), ((), ())), preferred_element_type=F32)


def dot_nt(a, b):
    return dot(a, b, 1, 1)


def dot_tn(a, b):
    return dot(a, b, 0, 0)


def half(v):
    return v.astype(BF)


def norm(v):
    c = v - jnp.mean(v, axis=-1, keepdims=True)
    inv = lax.rsqrt(jnp.mean(c * c, axis=-1, keepdims=True) + EPS)
    return c * inv, inv


def norm_back(g, gain, n, inv):
    gg = jnp.sum(g * n, axis=0, keepdims=True)
    inner = g * gain
    m1 = jnp.mean(inner, axis=-1, keepdims=True)
    m2 = jnp.mean(inner * n, axis=-1, keepdims=True)
    return inv * (inner - m1 - n * m2), gg


C0, C1 = 0.7978845608028654, 0.044715


def gelu(x):
    return 0.5 * x * (1.0 + jnp.tanh(C0 * (x + C1 * x * x * x)))


def gelu_slope(x):
    t = jnp.tanh(C0 * (x + C1 * x * x * x))
    return 0.5 * (1.0 + t) + 0.5 * x * (1.0 - t * t) * (C0 * (1.0 + 3.0 * C1 * x * x))


def lanes(width):
    return lax.broadcasted_iota(jnp.int32, (1, width), 1)


def head_mask(h):
    lane = lanes(256)
    return jnp.where((lane >= OFF[h]) & (lane < OFF[h] + E), 1.0, 0.0).astype(F32)


def pieces(row, count):
    out = []
    done = 0
    while done < count:
        i, r0 = divmod(row + done, ROWS_I)
        n = min(count - done, ROWS_I - r0)
        out.append((i, r0, done, n))
        done += n
    return out


def split3(v):
    hi = half(v).astype(F32)
    mid = half(v - hi).astype(F32)
    lo = half(v - hi - mid).astype(F32)
    return hi, mid, lo


def pack3(v):
    hi, mid, lo = split3(v)
    return half(hi + pltpu.roll(mid, 16, 1) + pltpu.roll(lo, 32, 1))


def unpack3(v, axis):
    return v + pltpu.roll(v, 112, axis) + pltpu.roll(v, 96, axis)


def as_rows(parts, count):
    row = lax.broadcasted_iota(jnp.int32, (count, 128), 0)
    out = jnp.zeros((count, 128), F32)
    for r, part in parts:
        out = jnp.where(row == r, part, out)
    return out


def call(body, outs, args, scratch=(), vmem=48, flops=0, name=None):
    spaces = {"v": pltpu.VMEM, "a": pl.ANY, "s": pltpu.SMEM}
    return pl.pallas_call(
        body,
        out_shape=[jax.ShapeDtypeStruct(s, t) for s, t, _ in outs],
        in_specs=[pl.BlockSpec(memory_space=spaces[m]) for _, m in args],
        out_specs=[pl.BlockSpec(memory_space=spaces[m]) for _, _, m in outs],
        scratch_shapes=list(scratch),
        compiler_params=pltpu.CompilerParams(vmem_limit_bytes=vmem * MIB),
        cost_estimate=pl.CostEstimate(flops=int(flops), bytes_accessed=4 * MIB, transcendentals=0),
        name=name,
    )(*[a for a, _ in args])


DMA = pltpu.SemaphoreType.DMA


def pack_body(sc, lm, om, bm, do, la, g0, wsh, sem):
    i, core = sc[0], sc[4]
    cols = pl.ds(pl.multiple_of(core * 640, 128), 640)
    first = [
        pltpu.make_async_copy(bm.at[0, :, cols], g0.at[0:48, :], sem.at[8]),
        pltpu.make_async_copy(bm.at[1, :, cols], g0.at[48:96, :], sem.at[9]),
        pltpu.make_async_copy(lm.at[0, :, cols], g0.at[96:176, :], sem.at[10]),
        pltpu.make_async_copy(la.at[:, cols], g0.at[176:192, :], sem.at[11]),
    ]
    for c in first:
        c.start()
    blocks = [(80 * k, 80, (om if s == "o" else lm), n, D) for k, (s, n) in enumerate(SQUARE)]
    blocks += [(DEC_ROW, 80, do, None, DI), (BQ_ROW, 48, bm, 2, D)]
    for k in range(NI):
        lo, hi = ROWS_I * k, ROWS_I * (k + 1)

        @pl.when(i == k)
        def _(lo=lo, hi=hi):
            cs = []
            for row, count, ref, n, width in blocks:
                a, b = max(lo, row), min(hi, row + count)
                if a < b:
                    src = ref.at[a - row : b - row, :] if n is None else ref.at[n, a - row : b - row, :]
                    dst = wsh.at[a - lo : b - lo, :] if width == D else wsh.at[a - lo : b - lo, 0:width]
                    cs.append(pltpu.make_async_copy(src, dst, sem.at[len(cs)]))
            for c in cs:
                c.start()
            for c in cs:
                c.wait()

    for c in first:
        c.wait()


def enc_body(sc, t0, t1, t2, t3, u0, u1, u2, u3, x_in, bg, lg, g_out, nb_o, k_o, v_o, q_o, z_o, pay, gs, acc, sem):
    x, z, core = sc[2], sc[3], sc[4]
    copies = []
    for side, group in enumerate(((t0, t1, t2, t3), (u0, u1, u2, u3))):
        c = core if side == 0 else 1 - core
        col = pl.ds(pl.multiple_of(c * 640, 128), 640)
        for e in range(4):
            for d in range(4):
                xs = jnp.where(c == 0, (x + 4 - d) & 3, (x + 4 - e) & 3)
                zs = jnp.where(c == 0, (z + 4 - e) & 3, (z + 4 - d) & 3)
                copies.append(
                    pltpu.make_async_copy(group[e].at[d], gs.at[xs * 4 + zs, :, col], sem.at[len(copies)])
                )
    for c in copies:
        c.start()
    n_in, _ = norm(x_in[...].astype(F32))
    nb = half(n_in * bg[0:1, :])
    nb_o[...] = nb
    for c in copies:
        c.wait()
    save = pltpu.make_async_copy(gs, g_out, sem.at[32])
    save.start()
    k_o[...] = half(dot(nb, gs[:, 0:48, :].reshape(DI, D)))
    v_o[...] = half(dot(nb, gs[:, 48:96, :].reshape(DI, D)))
    z0b = gs[:, 176:192, :].reshape(R, D)
    z_o[...] = z0b
    nq, _ = norm(z0b.astype(F32))
    q_o[...] = half(dot(half(nq * lg[0:1, :]), gs[:, 96:176, :].reshape(D, D)))
    acc[...] = jnp.zeros_like(acc)
    valid = lanes(N) + sc[1] * N < sc[5]
    lane = lanes(128)
    stats = jnp.zeros((R, 128), F32)
    for h in range(H):
        w = slice(WIN[h], WIN[h] + 256)
        mk = head_mask(h)
        s = dot_nt(q_o[:, w] * half(mk), k_o[:, w]) * SCALE
        s = jnp.where(valid, s, -1e30)
        m = jnp.max(s, axis=-1, keepdims=True)
        p = jnp.exp(s - m)
        acc[:, w] += dot(half(p), v_o[:, w]) * mk
        stats = jnp.where(lane == h, m, stats)
        stats = jnp.where(lane == 8 + h, jnp.sum(p, axis=-1, keepdims=True), stats)
    pay[:, 0:D] = half(acc[...])
    pay[:, D : D + 128] = pack3(stats)
    save.wait()


def combine_body(rcv, out):
    st = unpack3(rcv[:, :, D : D + 128].astype(F32), 2)
    peak = jnp.max(st, axis=0, keepdims=True)
    w = jnp.exp(st - peak)
    total = jnp.sum(w * pltpu.roll(st, 120, 2), axis=0, keepdims=True)
    coef = w / total
    lane = lax.broadcasted_iota(jnp.int32, (1, 1, 128), 2)
    for t in range(10):
        h0, h1 = 128 * t // E, (128 * t + 127) // E
        c = coef[:, :, h0 : h0 + 1]
        if h1 != h0:
            c = jnp.where(lane >= E * h1 - 128 * t, coef[:, :, h1 : h1 + 1], c)
        o = jnp.sum(rcv[:, :, 128 * t : 128 * t + 128].astype(F32) * c, axis=0)
        out[:, 128 * t : 128 * t + 128] = half(o)
    lse = jnp.where(lanes(128) < 8, (peak + jnp.log(total))[0], 0.0)
    out[:, D : D + 128] = pack3(lse)


class Ring:
    def __init__(self, w, slots, sem, order):
        self.w, self.slots, self.sem, self.order = w, slots, sem, order
        self.n = slots.shape[0]
        self.pos = {m: k for k, m in enumerate(order)}

    def copies(self, m):
        s = self.pos[m] % self.n
        return [
            pltpu.make_async_copy(
                self.w.at[i, :, r0 : r0 + n, :], self.slots.at[s, :, d0 : d0 + n, :], self.sem.at[s, k]
            )
            for k, (i, r0, d0, n) in enumerate(pieces(80 * m, 80))
        ]

    def start(self, m):
        for c in self.copies(m):
            c.start()

    def begin(self):
        for m in self.order[: self.n]:
            self.start(m)

    def get(self, m):
        for c in self.copies(m):
            c.wait()
        return self.slots[self.pos[m] % self.n].reshape(D, D)

    def done(self, m):
        k = self.pos[m] + self.n
        if k < len(self.order):
            self.start(self.order[k])


def lat_forward_body(e, z0b, lg, w, kd, vd, z_h, h_h, a_h, slots, zs, hs, qs, acc, wsem, ssem):
    ring = Ring(w, slots, wsem, list(range(11)))
    ring.begin()
    saves = []

    def save(src, dst):
        c = pltpu.make_async_copy(src, dst, ssem.at[len(saves)])
        c.start()
        saves.append(c)

    def mul(a, m):
        out = dot(a, ring.get(m))
        ring.done(m)
        return out

    z1 = z0b[...].astype(F32) + mul(e[:, 0:D], 0)
    zs[0] = z1
    save(zs.at[0], z_h.at[0])
    h1 = mul(half(norm(z1)[0] * lg[1:2, :]), 1)
    hs[0] = h1
    save(hs.at[0], h_h.at[0])
    zs[1] = zs[0] + mul(half(gelu(h1)), 2)
    save(zs.at[1], z_h.at[1])
    s_b = half(norm(zs[1])[0] * lg[2:3, :])
    for k in range(3):
        qs[k] = half(mul(s_b, 3 + k))
        save(qs.at[k], a_h.at[k])
    acc[...] = jnp.zeros_like(acc)
    for h in range(H):
        win = slice(WIN[h], WIN[h] + 256)
        mk = head_mask(h)
        s = dot_nt(qs[0, :, win] * half(mk), qs[1, :, win]) * SCALE
        p = jnp.exp(s - jnp.max(s, axis=-1, keepdims=True))
        p = p / jnp.sum(p, axis=-1, keepdims=True)
        acc[:, win] += dot(half(p), qs[2, :, win]) * mk
    qs[3] = half(acc[...])
    save(qs.at[3], a_h.at[3])
    zs[2] = zs[1] + mul(qs[3], 6)
    save(zs.at[2], z_h.at[2])
    h2 = mul(half(norm(zs[2])[0] * lg[3:4, :]), 7)
    hs[1] = h2
    save(hs.at[1], h_h.at[1])
    zs[3] = zs[2] + mul(half(gelu(h2)), 8)
    save(zs.at[3], z_h.at[3])
    c_b = half(norm(zs[3])[0] * lg[4:5, :])
    kd[...] = half(mul(c_b, 9))
    vd[...] = half(mul(c_b, 10))
    for c in saves:
        c.wait()


def lat_backward_body(
    sc, e, gkv, lg, w, z_h, h_h, a_h, gmix, pack_o, g1c_o, gains_o, slots, zs, hs, qs, gs, acc, acc2, acc3, pack, wsem, ssem
):
    order = [9, 10, 8, 7, 6, 3, 4, 5, 2, 1, 0]
    ring = Ring(w, slots, wsem, order)
    loads = {}
    for k in (3, 2, 1, 0):
        loads["z", k] = pltpu.make_async_copy(z_h.at[k], zs.at[k], ssem.at[k])
        if k in (3, 2):
            loads["h", k - 2] = pltpu.make_async_copy(h_h.at[k - 2], hs.at[k - 2], ssem.at[k + 2])
    for k in range(4):
        loads["a", k] = pltpu.make_async_copy(a_h.at[k], qs.at[k], ssem.at[6 + k])
    loads["z", 3].start()
    ring.begin()
    loads["h", 1].start()
    loads["z", 2].start()
    for k in range(4):
        loads["a", k].start()
    for key in (("z", 1), ("h", 0), ("z", 0)):
        loads[key].start()
    pack[...] = jnp.zeros_like(pack)
    src = sc[1] * 80
    start = jnp.minimum((src >> 7) * 128, 1024)
    start = pl.multiple_of(start, 128)
    offset = src - start

    def window(target):
        v = gs[:, pl.ds(start, 256)]
        return pltpu.roll(v, (target - offset + 256) & 255, 1)

    lane = lanes(256)

    def weight_grad(a_b, g, m):
        gs[...] = g
        base = 128 * (80 * m // 128)
        to = 80 * m - base
        wide = 128 if to + 80 <= 128 else 256
        v = jnp.where((lane >= to) & (lane < to + 80), window(to), 0.0)
        pack[:, base : base + wide] += dot_tn(a_b, half(v[:, 0:wide]))

    def mul(g_b, m):
        out = dot_nt(g_b, ring.get(m))
        ring.done(m)
        return out

    gain_rows = []

    def gain(k, gg):
        for t in range(10):
            gain_rows.append((10 * (k - 1) + t, gg[:, 128 * t : 128 * t + 128]))

    gk = gkv[:, 0:D]
    gv = gkv[:, D : 2 * D]
    loads["z", 3].wait()
    n, inv = norm(zs[3])
    c_b = half(n * lg[4:5, :])
    weight_grad(c_b, gk.astype(F32), 9)
    weight_grad(c_b, gv.astype(F32), 10)
    gn = mul(gk, 9) + mul(gv, 10)
    g4, gg = norm_back(gn, lg[4:5, :], n, inv)
    gain(4, gg)
    acc[...] = g4
    loads["h", 1].wait()
    weight_grad(half(gelu(hs[1])), g4, 8)
    gh = mul(half(g4), 8) * gelu_slope(hs[1])
    loads["z", 2].wait()
    n, inv = norm(zs[2])
    weight_grad(half(n * lg[3:4, :]), gh, 7)
    g3, gg = norm_back(mul(half(gh), 7), lg[3:4, :], n, inv)
    gain(3, gg)
    acc[...] += g3
    g3 = acc[...]
    for k in range(4):
        loads["a", k].wait()
    weight_grad(qs[3], g3, 6)
    qs[4] = half(mul(half(g3), 6))
    acc2[...] = jnp.zeros_like(acc2)
    for k in range(2):
        acc3[k] = jnp.zeros_like(acc2)
    for h in range(H):
        win = slice(WIN[h], WIN[h] + 256)
        mk = head_mask(h)
        mkb = half(mk)
        s = dot_nt(qs[0, :, win] * mkb, qs[1, :, win]) * SCALE
        p = jnp.exp(s - jnp.max(s, axis=-1, keepdims=True))
        p = p / jnp.sum(p, axis=-1, keepdims=True)
        dp = dot_nt(qs[4, :, win] * mkb, qs[2, :, win])
        ds = half(p * (dp - jnp.sum(p * dp, axis=-1, keepdims=True)))
        acc2[:, win] += dot(ds, qs[1, :, win]) * mk
        acc3[0, :, win] += dot_tn(ds, qs[0, :, win]) * mk
        acc3[1, :, win] += dot_tn(half(p), qs[4, :, win]) * mk
    loads["z", 1].wait()
    n, inv = norm(zs[1])
    s_b = half(n * lg[2:3, :])
    gq = acc2[...] * SCALE
    weight_grad(s_b, gq, 3)
    gn = mul(half(gq), 3)
    gk = acc3[0] * SCALE
    weight_grad(s_b, gk, 4)
    gn = gn + mul(half(gk), 4)
    weight_grad(s_b, acc3[1], 5)
    gn = gn + mul(half(acc3[1]), 5)
    g2, gg = norm_back(gn, lg[2:3, :], n, inv)
    gain(2, gg)
    acc[...] += g2
    g2 = acc[...]
    loads["h", 0].wait()
    weight_grad(half(gelu(hs[0])), g2, 2)
    gh = mul(half(g2), 2) * gelu_slope(hs[0])
    loads["z", 0].wait()
    n, inv = norm(zs[0])
    weight_grad(half(n * lg[1:2, :]), gh, 1)
    g1, gg = norm_back(mul(half(gh), 1), lg[1:2, :], n, inv)
    gain(1, gg)
    acc[...] += g1
    g1 = acc[...]
    weight_grad(e[:, 0:D], g1, 0)
    g1c_o[...] = half(window(0)[:, 0:128])
    gmix[...] = half(mul(half(g1), 0))
    gains_o[...] = as_rows(gain_rows, 48)
    pack_o[...] = half(pack[...])


def dec_body(qin, cot, bg, kd, vd, w, res, gqin, pay, gain_o, mix_o, nd_o, gq_o, dec, bq, acc, gq, gkv, sem):
    copies = []
    for i, r0, d0, n in pieces(DEC_ROW, 80):
        copies.append(
            pltpu.make_async_copy(w.at[i, :, r0 : r0 + n, 0:DI], dec.at[:, d0 : d0 + n, :], sem.at[len(copies)])
        )
    for i, r0, d0, n in pieces(BQ_ROW, 48):
        copies.append(
            pltpu.make_async_copy(w.at[i, :, r0 : r0 + n, :], bq.at[:, d0 : d0 + n, :], sem.at[len(copies)])
        )
    for c in copies:
        c.start()
    x = qin[...].astype(F32)
    n, inv = norm(x)
    nd = half(n * bg[1:2, :])
    nd_o[...] = nd
    for c in copies:
        c.wait()
    wq = bq[...].reshape(DI, D)
    wd = dec[...].reshape(D, DI)
    gq_o[...] = half(dot(nd, wq))
    gq[...] = dot_nt(cot[...], wd)
    gm = half(gq[...])
    mix_o[...] = gm
    acc[...] = jnp.zeros_like(acc)
    gq[...] = jnp.zeros_like(gq)
    gkv[...] = jnp.zeros_like(gkv)
    for h in range(H):
        win = slice(WIN[h], WIN[h] + 256)
        mk = head_mask(h)
        mkb = half(mk)
        qw, gw, kw, vw = gq_o[:, win], mix_o[:, win], kd[:, win], vd[:, win]
        s = dot_nt(qw * mkb, kw) * SCALE
        p = jnp.exp(s - jnp.max(s, axis=-1, keepdims=True))
        p = p / jnp.sum(p, axis=-1, keepdims=True)
        pb = half(p)
        acc[:, win] += dot(pb, vw) * mk
        dp = dot_nt(gw * mkb, vw)
        ds = half(p * (dp - jnp.sum(p * dp, axis=-1, keepdims=True)))
        gq[:, win] += dot(ds, kw) * mk
        gkv[0, :, win] += dot_tn(ds, qw) * mk
        gkv[1, :, win] += dot_tn(pb, gw) * mk
    pay[:, 0:D] = half(gkv[0] * SCALE)
    pay[:, D : 2 * D] = half(gkv[1])
    mix = half(acc[...])
    mix_o[...] = mix
    res[...] = half(x + dot(mix, wd))
    gqb = half(gq[...] * SCALE)
    gq_o[...] = gqb
    gin, gg = norm_back(dot_nt(gqb, wq), bg[1:2, :], n, inv)
    gqin[...] = cot[...].astype(F32) + gin
    gain_o[...] = gg


def sum_rows_body(rcv, out):
    s = half(jnp.sum(rcv[...].astype(F32), axis=0))
    for k in range(NJ):
        out[k] = s


def dec_weights_body(mix, cot, nd, gq, out):
    g = half(dot_tn(mix[...], cot[...]))
    for i in range(NI):
        for t in range(6):
            out[i, 160 * t : 160 * t + 160, :] = g[160 * i : 160 * i + 160, 128 * t : 128 * t + 128]
    g = half(dot_tn(nd[...], gq[...]))
    for i in range(NI):
        for t in range(10):
            r = 960 + 96 * t
            out[i, r : r + 96, :] = g[96 * i : 96 * i + 96, 128 * t : 128 * t + 128]


def dec_spread_body(chunk, out, td, tb):
    fill = jnp.zeros((96, 128), F32)
    for t in range(6):
        v = jnp.concatenate([chunk[160 * t : 160 * t + 160, :].astype(F32), fill], axis=0)
        td[128 * t : 128 * t + 128, :] = v.T
    fill = jnp.zeros((32, 128), F32)
    for t in range(10):
        v = jnp.concatenate([chunk[960 + 96 * t : 960 + 96 * t + 96, :].astype(F32), fill], axis=0)
        tb[128 * t : 128 * t + 128, :] = v.T
    for j in range(NJ):
        out[j, 0:48, :] = half(td[48 * j : 48 * j + 48, 0:128])
        out[j, 48:96, :] = half(td[48 * j : 48 * j + 48, 128:256])
        out[j, 96:176, :] = half(tb[80 * j : 80 * j + 80, :])


def dec_finish_body(rcv, dec_o, bq_o):
    s = jnp.sum(rcv[...].astype(F32), axis=0)
    fill = jnp.zeros((80, 128), F32)
    a = jnp.concatenate([s[0:48], fill], axis=0).T
    b = jnp.concatenate([s[48:96], fill], axis=0).T
    dec_o[0:128, :] = a[:, 0:48]
    dec_o[128:160, :] = b[0:32, 0:48]
    c = jnp.concatenate([s[96:176], fill[0:48]], axis=0).T
    bq_o[...] = c[0:96, 0:80]


def enc_back_body(sc, gmix, e, q, k, v, x_in, bg, gd, g_all, gin_o, pay, wkv, gq, gkt, gvt, sem):
    load = pltpu.make_async_copy(g_all.at[:, 0:96, :], wkv, sem)
    load.start()
    lse = unpack3(e[:, D : D + 128].astype(F32), 1)
    valid = lanes(N) + sc[1] * N < sc[5]
    gq[...] = jnp.zeros_like(gq)
    for h in range(H):
        win = slice(WIN[h], WIN[h] + 256)
        mk = head_mask(h)
        mkb = half(mk)
        qw, gw, kw, vw = q[:, win], gmix[:, win], k[:, win], v[:, win]
        rd = jnp.sum(gw.astype(F32) * e[:, win].astype(F32) * mk, axis=-1, keepdims=True)
        s = dot_nt(qw * mkb, kw) * SCALE
        p = jnp.where(valid, jnp.exp(jnp.where(valid, s, -1e30) - lse[:, h : h + 1]), 0.0)
        dp = dot_nt(gw * mkb, vw)
        ds = half(p * (dp - rd))
        gq[:, win] += dot(ds, kw) * mk
        o = OFF[h]
        gkt[E * h : E * h + E, :] = half(dot_tn(qw, ds)[o : o + E, :] * SCALE)
        gvt[E * h : E * h + E, :] = half(dot_tn(gw, half(p))[o : o + E, :])
    for t in range(10):
        pay[:, 16 * t : 16 * t + 16, :] = half(gq[:, 128 * t : 128 * t + 128] * SCALE).reshape(NJ, 16, 128)
    pay[:, 160:240, :] = gkt[...].reshape(NJ, 80, 128)
    pay[:, 240:320, :] = gvt[...].reshape(NJ, 80, 128)
    n, inv = norm(x_in[...].astype(F32))
    load.wait()
    gnt = dot(wkv[:, 0:48, :].reshape(DI, D), gkt[...]) + dot(wkv[:, 48:96, :].reshape(DI, D), gvt[...])
    gin, gg = norm_back(gnt.T, bg[0:1, :], n, inv)
    gin_o[...] = gin
    rows = [(t, gg[:, 128 * t : 128 * t + 128]) for t in range(6)]
    rows += [(6 + t, gd[:, 128 * t : 128 * t + 128]) for t in range(6)]
    g = as_rows(rows, 16)
    hi = half(g)
    lo = half(g - hi.astype(F32))
    for j in range(NJ):
        pay[j, 320:336, :] = hi
        pay[j, 336:352, :] = lo


def tail_one_body(rcv, nf, lat_gain, g1c, out, left):
    gq = half(jnp.sum(rcv[:, 0:160, :].astype(F32), axis=0))
    left[...] = jnp.zeros_like(left)
    for s in range(NJ):
        left[0:80, 128 * s : 128 * s + 128] = rcv[s, 160:240, :]
        left[128:208, 128 * s : 128 * s + 128] = rcv[s, 240:320, :]
    wt = half(dot(left[...], nf[...]).T)
    b = jnp.sum(rcv[:, 320:352, :].astype(F32), axis=0)
    g = jnp.concatenate([b[0:16] + b[16:32], lat_gain[...]], axis=0)
    hi = half(g)
    lo = half(g - hi.astype(F32))
    for i in range(NI):
        out[i, 0:160, :] = gq
        out[i, 160:256, :] = wt[96 * i : 96 * i + 96, 0:128]
        out[i, 256:352, :] = wt[96 * i : 96 * i + 96, 128:256]
        out[i, 352:416, :] = hi
        out[i, 416:480, :] = lo
        out[i, 480:512, :] = g1c[32 * i : 32 * i + 32, :]


def tail_two_body(sc, rcv, z0b, lg, g_all, pay, wkv_o, byte_o, lat_o, g1s_o, w0, sem):
    load = pltpu.make_async_copy(g_all.at[:, 96:176, :], w0, sem)
    load.start()
    sums = jnp.sum(rcv[...].astype(F32), axis=0)
    wkv_o[0] = sums[160:256, 0:80]
    wkv_o[1] = sums[256:352, 0:80]
    g = sums[352:416] + sums[416:480]
    for t in range(6):
        for b in range(2):
            byte_o[b : b + 1, 128 * t : 128 * t + 128] = g[6 * b + t : 6 * b + t + 1, :]
    for t in range(10):
        for b in range(4):
            r = 16 + 10 * b + t
            lat_o[b : b + 1, 128 * t : 128 * t + 128] = g[r : r + 1, :]
    g1s_o[...] = sums[480:512]
    sg = jnp.concatenate([sums[16 * t : 16 * t + 16, :] for t in range(10)], axis=1)
    n, inv = norm(z0b[pl.ds(pl.multiple_of(sc[1] * 16, 16), 16), :].astype(F32))
    load.wait()
    gz, gg = norm_back(dot_nt(half(sg), w0[...].reshape(D, D)), lg[0:1, :], n, inv)
    g = as_rows([(t, gg[:, 128 * t : 128 * t + 128]) for t in range(10)], 16)
    hi = half(g)
    lo = half(g - hi.astype(F32))
    for j in range(NJ):
        s = min(128 * (80 * j // 128), 1024)
        o = 80 * j - s
        a, b = gz[:, s : s + 256], sg[:, s : s + 256]
        if o:
            a, b = pltpu.roll(a, 256 - o, 1), pltpu.roll(b, 256 - o, 1)
        pay[j, 0:16, :] = half(a[:, 0:128])
        pay[j, 16:32, :] = half(b[:, 0:128])
        pay[j, 32:48, :] = hi
        pay[j, 48:64, :] = lo


def tail_three_body(sc, rcv, z0b, lg, g1s, lat, pack, arr_o, lm_o, om_o, gain_o, w0):
    i = sc[0]
    nq = half(norm(z0b[...].astype(F32))[0] * lg[0:1, :])
    w0[...] = dot_tn(nq, rcv[:, 16:32, :].reshape(R, 128))
    lm_o[0] = w0[pl.ds(pl.multiple_of(i * 160, 32), 160), :][:, 0:80]
    gz = jnp.concatenate([rcv[2 * i, 0:16, :].astype(F32), rcv[2 * i + 1, 0:16, :].astype(F32)], axis=0)
    arr_o[...] = (gz + g1s[...])[:, 0:80]
    g = jnp.sum(rcv[:, 32:64, :].astype(F32), axis=0)
    g = g[0:16] + g[16:32]
    for t in range(10):
        gain_o[0:1, 128 * t : 128 * t + 128] = g[t : t + 1, :]
    gain_o[1:5, :] = lat[...]
    for m, (kind, n) in enumerate(SQUARE):
        base = 128 * (80 * m // 128)
        o = 80 * m - base
        wide = 128 if o + 80 <= 128 else 256
        v = pack[:, base : base + wide].astype(F32)
        if o:
            v = pltpu.roll(v, wide - o, 1)
        if kind == "l":
            lm_o[n] = v[:, 0:80]
        else:
            om_o[n] = v[:, 0:80]


def line(y, c, x, z):
    return ((y % 4) * 2 + c) * NJ + (x % 4) * NZ + (z % 4)


EVERY = [(y, c, x, z) for y in range(4) for c in range(2) for x in range(NX) for z in range(NZ)]


def along(stage, d):
    out = []
    for y, c, x, z in EVERY:
        on_x = (c == 0) == (stage == 0)
        out.append((line(y, c, x, z), line(y, c, x + d, z) if on_x else line(y, c, x, z + d)))
    return out


SWAP = [(line(y, c, x, z), line(y, 1 - c, x, z)) for y, c, x, z in EVERY]


def exchange(v, axes):
    flat = v.reshape(v.shape[0] * v.shape[1], v.shape[2])
    return lax.all_to_all(flat, axes, split_axis=0, concat_axis=0, tiled=True).reshape(v.shape)


def shards(inputs, queries, lengths, latent_array, latent_mats, out_mats, byte_mats, dec_out, lg, bg, cotangent):
    y, core, x, z = (lax.axis_index(a) for a in AXES)
    i, j = y * 2 + core, x * NZ + z
    sc = jnp.stack([i, j, x, z, core, lengths[0]]).astype(jnp.int32)
    xin, qin, cot = inputs[0], queries[0], cotangent[0]

    g0, wsh = call(
        pack_body,
        [((192, 640), BF, "a"), ((ROWS_I, D), BF, "a")],
        [(sc, "s"), (latent_mats, "a"), (out_mats, "a"), (byte_mats, "a"), (dec_out, "a"), (latent_array, "a")],
        [DMA((12,))],
        vmem=16,
        name="pack",
    )
    w = lax.all_gather(wsh, AXES, axis=0, tiled=True).reshape(NI, NJ, ROWS_I, D)

    s1 = jnp.stack([g0] + [lax.ppermute(g0, AXES, along(0, d)) for d in (1, 2, 3)])
    own = [s1] + [lax.ppermute(s1, AXES, along(1, d)) for d in (1, 2, 3)]
    sib = [lax.ppermute(v, AXES, SWAP) for v in own]
    g_all, nb, k_b, v_b, q_b, z0b, pay = call(
        enc_body,
        [
            ((NJ, 192, D), BF, "a"),
            ((N, DI), BF, "v"),
            ((N, D), BF, "v"),
            ((N, D), BF, "v"),
            ((R, D), BF, "v"),
            ((R, D), BF, "v"),
            ((R, D + 128), BF, "v"),
        ],
        [(sc, "s")] + [(v, "a") for v in own + sib] + [(xin, "v"), (bg, "v"), (lg, "v")],
        [pltpu.VMEM((NJ, 192, D), BF), pltpu.VMEM((R, D), F32), DMA((33,))],
        flops=3e9,
        name="enc",
    )
    rcv = exchange(pay.reshape(NJ, 16, D + 128), BLK)
    (mine,) = call(combine_body, [((16, D + 128), BF, "v")], [(rcv, "v")], name="combine")
    e = lax.all_gather(mine, BLK, axis=0, tiled=True)
    nf = lax.all_gather(nb, BLK, axis=0, tiled=True)

    big = (NJ, 80, D)
    kd, vd, z_h, h_h, a_h = call(
        lat_forward_body,
        [
            ((R, D), BF, "v"),
            ((R, D), BF, "v"),
            ((4, R, D), F32, "a"),
            ((2, R, D), F32, "a"),
            ((4, R, D), BF, "a"),
        ],
        [(e, "v"), (z0b, "v"), (lg, "v"), (w, "a")],
        [
            pltpu.VMEM((5,) + big, BF),
            pltpu.VMEM((4, R, D), F32),
            pltpu.VMEM((2, R, D), F32),
            pltpu.VMEM((4, R, D), BF),
            pltpu.VMEM((R, D), F32),
            DMA((5, 2)),
            DMA((10,)),
        ],
        vmem=56,
        flops=1.2e10,
        name="lat_forward",
    )
    res, gqin, dpay, gd, mix, nd, gq = call(
        dec_body,
        [
            ((N, DI), BF, "v"),
            ((N, DI), F32, "v"),
            ((R, 2 * D), BF, "v"),
            ((1, DI), F32, "v"),
            ((N, D), BF, "v"),
            ((N, DI), BF, "v"),
            ((N, D), BF, "v"),
        ],
        [(qin, "v"), (cot, "v"), (bg, "v"), (kd, "v"), (vd, "v"), (w, "a")],
        [
            pltpu.VMEM((NJ, 80, DI), BF),
            pltpu.VMEM((NJ, 48, D), BF),
            pltpu.VMEM((N, D), F32),
            pltpu.VMEM((N, D), F32),
            pltpu.VMEM((2, R, D), F32),
            DMA((3,)),
        ],
        flops=3e9,
        name="dec",
    )
    rows = exchange(dpay.reshape(NJ, 16, 2 * D), BLK)
    (dup,) = call(sum_rows_body, [((NJ, 16, 2 * D), BF, "v")], [(rows, "v")], name="sum_rows")
    gkv = exchange(dup, BLK).reshape(R, 2 * D)
    (dw,) = call(
        dec_weights_body,
        [((NI, 1920, 128), BF, "v")],
        [(mix, "v"), (cot, "v"), (nd, "v"), (gq, "v")],
        flops=5e8,
        name="dec_weights",
    )
    dw = lax.psum_scatter(dw.reshape(NI * 1920, 128), BATCH, scatter_dimension=0, tiled=True)
    (dspread,) = call(
        dec_spread_body,
        [((NJ, 176, 128), BF, "v")],
        [(dw, "v")],
        [pltpu.VMEM((DI, 256), F32), pltpu.VMEM((D, 128), F32)],
        name="dec_spread",
    )
    dwr = exchange(dspread, BLK)
    dec_grad, bq_grad = call(
        dec_finish_body, [((160, 48), F32, "v"), ((96, 80), F32, "v")], [(dwr, "v")], name="dec_finish"
    )

    gmix, pack, g1c, lat_gain = call(
        lat_backward_body,
        [((R, D), BF, "v"), ((D, 896), BF, "v"), ((R, 128), BF, "v"), ((48, 128), F32, "v")],
        [(sc, "s"), (e, "v"), (gkv, "v"), (lg, "v"), (w, "a"), (z_h, "a"), (h_h, "a"), (a_h, "a")],
        [
            pltpu.VMEM((4,) + big, BF),
            pltpu.VMEM((4, R, D), F32),
            pltpu.VMEM((2, R, D), F32),
            pltpu.VMEM((5, R, D), BF),
            pltpu.VMEM((R, D), F32),
            pltpu.VMEM((R, D), F32),
            pltpu.VMEM((R, D), F32),
            pltpu.VMEM((2, R, D), F32),
            pltpu.VMEM((D, 896), F32),
            DMA((4, 2)),
            DMA((10,)),
        ],
        vmem=58,
        flops=1.6e10,
        name="lat_backward",
    )
    pack = lax.psum_scatter(pack, BATCH, scatter_dimension=0, tiled=True)
    gin, epay = call(
        enc_back_body,
        [((N, DI), F32, "v"), ((NJ, 352, 128), BF, "v")],
        [(sc, "s"), (gmix, "v"), (e, "v"), (q_b, "v"), (k_b, "v"), (v_b, "v"), (xin, "v"), (bg, "v"), (gd, "v"), (g_all, "a")],
        [
            pltpu.VMEM((NJ, 96, D), BF),
            pltpu.VMEM((R, D), F32),
            pltpu.VMEM((D, N), BF),
            pltpu.VMEM((D, N), BF),
            DMA,
        ],
        flops=2e9,
        name="enc_back",
    )
    r1 = exchange(epay, BLK)
    (p2,) = call(
        tail_one_body,
        [((NI, 512, 128), BF, "v")],
        [(r1, "v"), (nf, "v"), (lat_gain, "v"), (g1c, "v")],
        [pltpu.VMEM((256, 2048), BF)],
        name="tail_one",
    )
    r2 = exchange(p2, BATCH)
    p3, wkv, byte_gain, lat4, g1s = call(
        tail_two_body,
        [
            ((NJ, 64, 128), BF, "v"),
            ((2, 96, 80), F32, "v"),
            ((2, DI), F32, "v"),
            ((4, D), F32, "v"),
            ((32, 128), F32, "v"),
        ],
        [(sc, "s"), (r2, "v"), (z0b, "v"), (lg, "v"), (g_all, "a")],
        [pltpu.VMEM(big, BF), DMA],
        name="tail_two",
    )
    r3 = exchange(p3, BLK)
    arr, lm, om, lat_gains = call(
        tail_three_body,
        [((32, 80), F32, "v"), ((10, 160, 80), F32, "v"), ((2, 160, 80), F32, "v"), ((5, D), F32, "v")],
        [(sc, "s"), (r3, "v"), (z0b, "v"), (lg, "v"), (g1s, "v"), (lat4, "v"), (pack, "v")],
        [pltpu.VMEM((D, 128), F32)],
        name="tail_three",
    )
    byte_grads = jnp.concatenate([wkv, bq_grad[None]], axis=0)
    return (res[None], gin[None], gqin[None], arr, lm, om, byte_grads, dec_grad, lat_gains, byte_gain)


def solution(mesh):
    grid = Mesh(mesh.devices.reshape(4, 2, NX, NZ), AXES)
    return jax.shard_map(
        shards,
        mesh=grid,
        in_specs=(
            P(BATCH, BLK, None),
            P(BATCH, BLK, None),
            P(BATCH),
            P(BLK, None),
            P(None, BLK, None),
            P(None, BLK, None),
            P(None, BLK, None),
            P(BLK, None),
            P(),
            P(),
            P(BATCH, BLK, None),
        ),
        out_specs=(
            P(BATCH, BLK, None),
            P(BATCH, BLK, None),
            P(BATCH, BLK, None),
            P(BATCH, BLK),
            P(None, BATCH, BLK),
            P(None, BATCH, BLK),
            P(None, BATCH, BLK),
            P(BATCH, BLK),
            P(),
            P(),
        ),
        check_vma=False,
    )
```

time: 1110 us -> 388 us (0.35)
  the two profiles are of different devices: /device:TPU:1 before, /device:TPU:0 now
where the time goes in v1:
time: 388 us; the launch traced here: 381 us
  blocking collectives  118 us (30%)
  waiting for transfers between devices  114 us (29%)
  Pallas kernels  92.8 us (24%)
  starting transfers between devices  23 us (6%)
  local copies, waits for them, and re-layouts  17.8 us (5%)
  between operations  15.2 us (4%)
    pallas_call x14, Pallas kernels, call(): pl.pallas_call(body, out_shape=[jax.ShapeDtypeStruct(s, t) for s, t, _ in...  92.8 us
    all_to_all x4, blocking collectives, exchange(): lax.all_to_all(flat, axes, split_axis=0, concat_axis=0, tiled=True)  91.5 us
    all_gather x1, waiting for transfers between devices, shards(): w = lax.all_gather(wsh, AXES, axis=0, tiled=True).reshape(NI, NJ, ROWS_I, D)  42.1 us
    all_to_all x3, waiting for transfers between devices, exchange(): lax.all_to_all(flat, axes, split_axis=0, concat_axis=0, tiled=True)  35.3 us
    all_gather x1, blocking collectives, shards(): e = lax.all_gather(mine, BLK, axis=0, tiled=True)  26.9 us
    ppermute x3, waiting for transfers between devices, shards(): own = [s1] + [lax.ppermute(s1, AXES, along(1, d)) for d in (1, 2, 3)]  23.9 us
    unnamed x62, local copies, waits for them, and re-layouts  17.7 us
    all_to_all x3, starting transfers between devices, exchange(): lax.all_to_all(flat, axes, split_axis=0, concat_axis=0, tiled=True)  11.2 us
  transfers between devices with their start and end apart: 17, of which 11 were waited for; matrix products, arithmetic and copies ran while one was open for 0% of the time, Pallas kernels for 24%

profile of v1, /device:TPU:0, one launch (start us, length us, event | category | flops | bytes accessed | tf_op | source)
XLA Modules:
  0.0 380.9 jit_solution(6297353422692442702)
XLA Ops:
  14.7 2.9 collective-permute-start.2
  19.3 4.7 %collective-permute-done.2 = bf16[192,640]{1,0:T(8,128)(2,1)S(1)} collective-permute-done((bf16[192,640]{1,0:T(8,128)(2,1)S(1)}, bf16[192,640]{1,0:T(8,128)(2,1)S(1)}, u32[]{:S(2)}, u32[]{:S(2)}) %collective-permute-start.2) | collective-permute-done | bytes 245792 | tf_op jit(solution)/shard_map/ppermute | solution.py:689
  25.4 2.5 collective-permute-done
  30.1 3.6 collective-permute-start.4
  34.7 11.9 %collective-permute-done.3.t1 = bf16[4,192,640]{2,1,0:T(8,128)(2,1)S(1)} collective-permute-done((bf16[4,192,640]{2,1,0:T(8,128)(2,1)S(1)}, bf16[4,192,640]{2,1,0:T(8,128)(2,1)S(1)}, u32[]{:S(2)}, u32[]{:S(2)}) %collective-permute-start.3) | collective-permute-done | bytes 983072 | tf_op jit(solution)/shard_map/ppermute | solution.py:690
  46.6 12.0 %collective-permute-done.4.t2 = bf16[4,192,640]{2,1,0:T(8,128)(2,1)S(1)} collective-permute-done((bf16[4,192,640]{2,1,0:T(8,128)(2,1)S(1)}, bf16[4,192,640]{2,1,0:T(8,128)(2,1)S(1)}, u32[]{:S(2)}, u32[]{:S(2)}) %collective-permute-start.4) | collective-permute-done | bytes 983072 | tf_op jit(solution)/shard_map/ppermute | solution.py:690
  63.6 8.4 %enc.1 = (bf16[16,192,1280]{2,1,0:T(8,128)(2,1)}, bf16[128,768]{1,0:T(8,128)(2,1)}, bf16[128,1280]{1,0:T(8,128)(2,1)S(1)}, bf16[128,1280]{1,0:T(8,128)(2,1)S(1)}...) custom-call(s32[6]{0:T(128)S(1)} %stack.38.sc, ...), custom_call_target="tpu_custom_call" | custom-call | flops 3000000000 | bytes 4194304 | tf_op jit(solution)/shard_map/enc/pallas_call | solution.py:112
  72.9 19.0 %all_to_all.50.rcv = bf16[16,16,1408]{2,1,0:T(8,128)(2,1)S(1)} all-to-all(bf16[16,16,1408]{2,1,0:T(8,128)(2,1)S(1)} %bitcast.25), channel_id=1, replica_groups=mesh['y'=4,'core'=2,'x'=4,'z'=4] {'x','z'}, dimensions={0} | all-to-all | bytes 1441792 | tf_op jit(solution)/shard_map/all_to_all | solution.py:670
  92.5 26.9 %all_gather.9.e = bf16[256,1408]{1,0:T(8,128)(2,1)} all-gather(bf16[16,1408]{1,0:T(8,128)(2,1)S(1)} %combine.1), channel_id=1, replica_groups=mesh['y'=4,'core'=2,'x'=4,'z'=4] {'x','z'}, dimensions={0}, use_global_device_ids=true | all-gather | bytes 765952 | tf_op jit(solution)/shard_map/all_gather | solution.py:710
  119.3 42.1 %all-gather.3.cloned.1.call-done = bf16[16384,1280]{1,0:T(8,128)(2,1)} async-done(((bf16[128,1280]{1,0:T(8,128)(2,1)}), bf16[16384,1280]{1,0:T(8,128)(2,1)}) %all-gather.3.cloned.1.call-update) | async-done | bytes 41943056 | tf_op jit(solution)/shard_map/all_gather | solution.py:687
  161.4 20.4 %lat_forward.1 = (bf16[256,1280]{1,0:T(8,128)(2,1)}, bf16[256,1280]{1,0:T(8,128)(2,1)}, f32[4,256,1280]{2,1,0:T(8,128)}, f32[2,256,1280]{2,1,0:T(8,128)}, bf16[4,256,1280]{2,1,0:T(8,128)(2,1)}) custom-call(bf16[256,1408]{1,0:T(8,128)(2,1)} %all_gather.9.e, bf16[256,1280]{1,0:T(8,128)(2,1)} %copy-done.3, f32[5,1280]{1,0:T(8,128)} %lg.9, ...), custom_call_target="tpu_custom_call" | custom-call | flops 12000000000 | bytes 4194304 | tf_op jit(solution)/shard_map/lat_forward/pallas_call | solution.py:112
  184.0 9.4 %dec.1 = (bf16[128,768]{1,0:T(8,128)(2,1)}, f32[128,768]{1,0:T(8,128)}, bf16[256,2560]{1,0:T(8,128)(2,1)S(1)}, f32[1,768]{1,0:T(1,128)S(1)}, bf16[128,1280]{1,0:...) custom-call(bf16[128,768]{1,0:T(8,128)(2,1)S(1)} %bitcast.27, ...), custom_call_target="tpu_custom_call" | custom-call | flops 3000000000 | bytes 4194304 | tf_op jit(solution)/shard_map/dec/pallas_call | solution.py:112
  196.6 28.7 %all_to_all.51.rcv = bf16[16,16,2560]{2,1,0:T(8,128)(2,1)S(1)} all-to-all(bf16[16,16,2560]{2,1,0:T(8,128)(2,1)S(1)} %bitcast.22), channel_id=1, replica_groups=mesh['y'=4,'core'=2,'x'=4,'z'=4] {'x','z'}, dimensions={0} | all-to-all | bytes 2621440 | tf_op jit(solution)/shard_map/all_to_all | solution.py:670
  225.6 23.4 %all_to_all.52 = bf16[16,16,2560]{2,1,0:T(8,128)(2,1)} all-to-all(bf16[16,16,2560]{2,1,0:T(8,128)(2,1)S(1)} %sum_rows.1), channel_id=1, replica_groups=mesh['y'=4,'core'=2,'x'=4,'z'=4] {'x','z'}, dimensions={0} | all-to-all | bytes 2621440 | tf_op jit(solution)/shard_map/all_to_all | solution.py:670
  249.0 34.2 %lat_backward.1 = (bf16[256,1280]{1,0:T(8,128)(2,1)}, bf16[1280,896]{1,0:T(8,128)(2,1)}, bf16[256,128]{1,0:T(8,128)(2,1)}, f32[48,128]{1,0:T(8,128)}) custom-call(s32[6]{0:T(128)} %copy-done.23, bf16[256,1408]{1,0:T(8,128)(2,1)} %all_gather.9.e, bf16[256,2560]{1,0:T(8,128)(2,1)} %bitcast.34, f32[5,1280]{1,0:T(8,128)} %lg.9, ...), custom_call_target="tpu_custom_call" | custom-call | flops 16000000000 | bytes 4194304 | tf_op jit(solution)/shard_map/lat_backward/pallas_call | solution.py:112
  284.6 7.9 %enc_back.1 = (f32[128,768]{1,0:T(8,128)}, bf16[16,352,128]{2,1,0:T(8,128)(2,1)}) custom-call(s32[6]{0:T(128)S(1)} %copy-done.24, bf16[256,1280]{1,0:T(8,128)(2,1)S(1)} %copy-done.7, bf16[256,1408]{1,0:T(8,128)(2,1)S(1)} %copy-done.2, bf16[256,1280]{1,0:T(8,128)(2,1)S(1)} %get-tuple-element.60.q, bf16[128,1280]{1,0:T(8,128)(2,1)S(1)} %get-tuple-element.61.k, ...), custom_call_target="tpu_custom_call" | custom-call | flops 2000000000 | bytes 4194304 | tf_op jit(solution)/shard_map/enc_back/pallas_call | solution.py:112
  292.5 3.9 %all-to-all-start.3 = ((bf16[16,352,128]{2,1,0:T(8,128)(2,1)}), bf16[16,352,128]{2,1,0:T(8,128)(2,1)S(1)}, u32[]{:S(2)}, u32[]{:S(2)}) async-start(bf16[16,352,128]{2,1,0:T(8,128)(2,1)} %get-tuple-element.67), calls=%async_computation.3 | async-start | bytes 2883584 | tf_op jit(solution)/shard_map/all_to_all | solution.py:670
  296.4 20.0 %all-to-all-done.3.rcv = bf16[16,352,128]{2,1,0:T(8,128)(2,1)S(1)} async-done(((bf16[16,352,128]{2,1,0:T(8,128)(2,1)}), bf16[16,352,128]{2,1,0:T(8,128)(2,1)S(1)}, u32[]{:S(2)}, u32[]{:S(2)}) %all-to-all-start.3) | async-done | bytes 1441824 | tf_op jit(solution)/shard_map/all_to_all | solution.py:670
  319.5 20.3 %all_to_all.53.rcv = bf16[8,512,128]{2,1,0:T(8,128)(2,1)S(1)} all-to-all(bf16[8,512,128]{2,1,0:T(8,128)(2,1)S(1)} %tail_one.1), channel_id=1, replica_groups=mesh['y'=4,'core'=2,'x'=4,'z'=4] {'y','core'}, dimensions={0} | all-to-all | bytes 2097152 | tf_op jit(solution)/shard_map/all_to_all | solution.py:670
  339.8 4.4 %tail_two.1 = (bf16[16,64,128]{2,1,0:T(8,128)(2,1)}, f32[2,96,80]{2,1,0:T(8,128)S(1)}, f32[2,768]{1,0:T(2,128)}, f32[4,1280]{1,0:T(4,128)S(1)}, f32[32,128]{1,0:T(8,128)S(1)}) custom-call(s32[6]{0:T(128)S(1)} %copy-done.24, bf16[8,512,128]{2,1,0:T(8,128)(2,1)S(1)} %all_to_all.53.rcv, bf16[256,1280]{1,0:T(8,128)(2,1)S(1)} %copy-done.4, ...), custom_call_target="tpu_custom_call" | custom-call | bytes 4194304 | tf_op jit(solution)/shard_map/tail_two/pallas_call | solution.py:112
  344.2 3.6 all-to-all-start.5
  350.1 6.3 %all-to-all-done.5.rcv = bf16[16,64,128]{2,1,0:T(8,128)(2,1)S(1)} async-done(((bf16[16,64,128]{2,1,0:T(8,128)(2,1)}), bf16[16,64,128]{2,1,0:T(8,128)(2,1)S(1)}, u32[]{:S(2)}, u32[]{:S(2)}) %all-to-all-start.5) | async-done | bytes 262176 | tf_op jit(solution)/shard_map/all_to_all | solution.py:670
  356.4 3.6 all-to-all-start.6
  363.2 9.0 %all-to-all-done.6.rcv = bf16[16,176,128]{2,1,0:T(8,128)(2,1)S(1)} async-done(((bf16[16,176,128]{2,1,0:T(8,128)(2,1)}), bf16[16,176,128]{2,1,0:T(8,128)(2,1)S(1)}, u32[]{:S(2)}, u32[]{:S(2)}) %all-to-all-start.6) | async-done | bytes 720928 | tf_op jit(solution)/shard_map/all_to_all | solution.py:670
  (98 shorter events, 36.5 us)
Async XLA Ops:
  7.2 154.2 %all-gather.3.cloned.1.call-start = ((), (), s32[]{:S(2)}) async-start(), calls=%async_computation.9 | async-start | bytes 42270720 | tf_op jit(solution)/shard_map/all_gather | solution.py:687
  13.2 49.4 %copy-start.23 = (s32[6]{0:T(128)}, s32[6]{0:T(128)S(1)}, u32[]{:S(2)}) copy-start(s32[6]{0:T(128)S(1)} %stack.38.sc) | copy-start | bytes 76
  13.2 50.4 %copy-start.15 = (bf16[1,128,768]{2,1,0:T(8,128)(2,1)S(1)}, bf16[1,128,768]{2,1,0:T(8,128)(2,1)}, u32[]{:S(2)}) copy-start(bf16[1,128,768]{2,1,0:T(8,128)(2,1)} %param.11) | copy-start | bytes 589828
  13.2 50.4 %copy-start.16 = (f32[5,1280]{1,0:T(8,128)S(1)}, f32[5,1280]{1,0:T(8,128)}, u32[]{:S(2)}) copy-start(f32[5,1280]{1,0:T(8,128)} %lg.9) | copy-start | bytes 76804
  13.2 50.4 %copy-start.22 = (f32[2,768]{1,0:T(2,128)S(1)}, f32[2,768]{1,0:T(2,128)}, u32[]{:S(2)}) copy-start(f32[2,768]{1,0:T(2,128)} %bg.5) | copy-start | bytes 18436
  14.7 281.7 %all-gather.5.cloned.1.call-start = ((), (), s32[]{:S(2)}) async-start(), calls=%async_computation.10 | async-start | bytes 3342336 | tf_op jit(solution)/shard_map/all_gather | solution.py:711
  14.7 9.3 %collective-permute-start.2 = (bf16[192,640]{1,0:T(8,128)(2,1)S(1)}, bf16[192,640]{1,0:T(8,128)(2,1)S(1)}, u32[]{:S(2)}, u32[]{:S(2)}) collective-permute-start(bf16[192,640]{1,0:T(8,128)(2,1)S(1)} %get-tuple-element.48), channel_id=1, source_target_pairs={{0,12},{1,13},{2,14},{3,15},{4,0},{5,1},{6,2},{7,3},{8,4},{9,5},{1... | collective-permute-start | bytes 737288 | tf_op jit(solution)/shard_map/ppermute | solution.py:689
  17.6 7.8 %collective-permute-start.1 = (bf16[192,640]{1,0:T(8,128)(2,1)S(1)}, bf16[192,640]{1,0:T(8,128)(2,1)S(1)}, u32[]{:S(2)}, u32[]{:S(2)}) collective-permute-start(bf16[192,640]{1,0:T(8,128)(2,1)S(1)} %get-tuple-element.48), channel_id=1, source_target_pairs={{0,8},{1,9},{2,10},{3,11},{4,12},{5,13},{6,14},{7,15},{8,0},{9,1},... | collective-permute-start | bytes 737288 | tf_op jit(solution)/shard_map/ppermute | solution.py:689
  18.4 9.5 %collective-permute-start = (bf16[192,640]{1,0:T(8,128)(2,1)S(1)}, bf16[192,640]{1,0:T(8,128)(2,1)S(1)}, u32[]{:S(2)}, u32[]{:S(2)}) collective-permute-start(bf16[192,640]{1,0:T(8,128)(2,1)S(1)} %get-tuple-element.48), channel_id=1, source_target_pairs={{0,4},{1,5},{2,6},{3,7},{4,8},{5,9},{6,10},{7,11},{8,12},{9,13},{1... | collective-permute-start | bytes 737288 | tf_op jit(solution)/shard_map/ppermute | solution.py:689
  28.1 18.5 %collective-permute-start.3 = (bf16[4,192,640]{2,1,0:T(8,128)(2,1)S(1)}, bf16[4,192,640]{2,1,0:T(8,128)(2,1)S(1)}, u32[]{:S(2)}, u32[]{:S(2)}) collective-permute-start(bf16[4,192,640]{2,1,0:T(8,128)(2,1)S(1)} %pad_maximum_fusion.t0), channel_id=1, source_target_pairs={{0,1},{1,2},{2,3},{3,0},{4,5},{5,6},{6,7},{7,4},{8,9},{9,10},{10,1... | collective-permute-start | bytes 2949128 | tf_op jit(solution)/shard_map/ppermute | solution.py:690
  30.1 28.5 %collective-permute-start.4 = (bf16[4,192,640]{2,1,0:T(8,128)(2,1)S(1)}, bf16[4,192,640]{2,1,0:T(8,128)(2,1)S(1)}, u32[]{:S(2)}, u32[]{:S(2)}) collective-permute-start(bf16[4,192,640]{2,1,0:T(8,128)(2,1)S(1)} %pad_maximum_fusion.t0), channel_id=1, source_target_pairs={{0,2},{1,3},{2,0},{3,1},{4,6},{5,7},{6,4},{7,5},{8,10},{9,11},{10,... | collective-permute-start | bytes 2949128 | tf_op jit(solution)/shard_map/ppermute | solution.py:690
  33.7 24.9 %collective-permute-start.5 = (bf16[4,192,640]{2,1,0:T(8,128)(2,1)S(1)}, bf16[4,192,640]{2,1,0:T(8,128)(2,1)S(1)}, u32[]{:S(2)}, u32[]{:S(2)}) collective-permute-start(bf16[4,192,640]{2,1,0:T(8,128)(2,1)S(1)} %pad_maximum_fusion.t0), channel_id=1, source_target_pairs={{0,3},{1,0},{2,1},{3,2},{4,7},{5,4},{6,5},{7,6},{8,11},{9,8},{10,9... | collective-permute-start | bytes 2949128 | tf_op jit(solution)/shard_map/ppermute | solution.py:690
  34.7 24.4 %collective-permute-start.6 = (bf16[4,192,640]{2,1,0:T(8,128)(2,1)S(1)}, bf16[4,192,640]{2,1,0:T(8,128)(2,1)S(1)}, u32[]{:S(2)}, u32[]{:S(2)}) collective-permute-start(bf16[4,192,640]{2,1,0:T(8,128)(2,1)S(1)} %pad_maximum_fusion.t0), channel_id=1, source_target_pairs={{0,16},{1,17},{2,18},{3,19},{4,20},{5,21},{6,22},{7,23},{8,24},{9,... | collective-permute-start | bytes 2949128 | tf_op jit(solution)/shard_map/ppermute | solution.py:691
  46.6 12.5 %collective-permute-start.7 = (bf16[4,192,640]{2,1,0:T(8,128)(2,1)S(1)}, bf16[4,192,640]{2,1,0:T(8,128)(2,1)S(1)}, u32[]{:S(2)}, u32[]{:S(2)}) collective-permute-start(bf16[4,192,640]{2,1,0:T(8,128)(2,1)S(1)} %collective-permute-done.3.t1), channel_id=1, source_target_pairs={{0,16},{1,17},{2,18},{3,19},{4,20},{5,21},{6,22},{7,23},{8,24},{9,... | collective-permute-start | bytes 2949128 | tf_op jit(solution)/shard_map/ppermute | solution.py:691
  58.6 2.6 collective-permute-start.8
  58.6 4.0 %collective-permute-start.9 = (bf16[4,192,640]{2,1,0:T(8,128)(2,1)S(1)}, bf16[4,192,640]{2,1,0:T(8,128)(2,1)S(1)}, u32[]{:S(2)}, u32[]{:S(2)}) collective-permute-start(bf16[4,192,640]{2,1,0:T(8,128)(2,1)S(1)} %collective-permute-done.5.t3), channel_id=1, source_target_pairs={{0,16},{1,17},{2,18},{3,19},{4,20},{5,21},{6,22},{7,23},{8,24},{9,... | collective-permute-start | bytes 2949128 | tf_op jit(solution)/shard_map/ppermute | solution.py:691
  72.8 275.0 %reduce-scatter.5.cloned.1.call-start = ((), (), s32[]{:S(2)}) async-start(), calls=%async_computation.12 | async-start | bytes 4423680 | tf_op jit(solution)/shard_map/reduce_scatter | solution.py:770
  196.6 163.4 %reduce-scatter.3.cloned.1.call-start = ((), (), s32[]{:S(2)}) async-start(), calls=%async_computation.11 | async-start | bytes 2580480 | tf_op jit(solution)/shard_map/reduce_scatter | solution.py:804
  292.4 24.0 %copy-start.19 = (bf16[256,128]{1,0:T(8,128)(2,1)S(1)}, bf16[256,128]{1,0:T(8,128)(2,1)}, u32[]{:S(2)}) copy-start(bf16[256,128]{1,0:T(8,128)(2,1)} %get-tuple-element.70.g1c) | copy-start | bytes 196612
  292.5 24.0 %copy-start.21 = (f32[48,128]{1,0:T(8,128)S(1)}, f32[48,128]{1,0:T(8,128)}, u32[]{:S(2)}) copy-start(f32[48,128]{1,0:T(8,128)} %get-tuple-element.69.lat_gain) | copy-start | bytes 73732
  292.5 24.0 %all-to-all-start.3 = ((bf16[16,352,128]{2,1,0:T(8,128)(2,1)}), bf16[16,352,128]{2,1,0:T(8,128)(2,1)S(1)}, u32[]{:S(2)}, u32[]{:S(2)}) async-start(bf16[16,352,128]{2,1,0:T(8,128)(2,1)} %get-tuple-element.67), calls=%async_computation.3 | async-start | bytes 2883584 | tf_op jit(solution)/shard_map/all_to_all | solution.py:670
  318.3 21.5 %copy-start.17 = (f32[5,1280]{1,0:T(8,128)S(1)}, f32[5,1280]{1,0:T(8,128)}, u32[]{:S(2)}) copy-start(f32[5,1280]{1,0:T(8,128)} %lg.9) | copy-start | bytes 76804
  344.2 12.2 %all-to-all-start.5 = ((bf16[16,64,128]{2,1,0:T(8,128)(2,1)}), bf16[16,64,128]{2,1,0:T(8,128)(2,1)S(1)}, u32[]{:S(2)}, u32[]{:S(2)}) async-start(bf16[16,64,128]{2,1,0:T(8,128)(2,1)} %get-tuple-element.71), calls=%async_computation.5 | async-start | bytes 524288 | tf_op jit(solution)/shard_map/all_to_all | solution.py:670
  356.4 15.9 %all-to-all-start.6 = ((bf16[16,176,128]{2,1,0:T(8,128)(2,1)}), bf16[16,176,128]{2,1,0:T(8,128)(2,1)S(1)}, u32[]{:S(2)}, u32[]{:S(2)}) async-start(bf16[16,176,128]{2,1,0:T(8,128)(2,1)} %dec_spread.1), calls=%async_computation.8 | async-start | bytes 1441792 | tf_op jit(solution)/shard_map/all_to_all | solution.py:670
  (23 other events, 92.2 us)
Sparse Core Ops, SparseCore 0:
  14.8 146.5 all-gather.2
  163.6 57.2 all-gather.4
  223.3 39.3 reduce-scatter.4
  283.4 32.4 reduce-scatter.2
